TPU v7x, 256 devices: a whole 4x4x8 slice. The times are simulated.
256 devices in a mesh: freq: 8 (over y, core), site: 32 (over z, x).
Axes of the slice: x: 4, y: 4, z: 8, core: 2. Of those that a mesh axis runs over, the one named last changes fastest.
Arguments:
- incident: float32 [512, 32, 2, 512], P('site', 'freq'), parts along dimension 1, may hold values from -6 to 6
- diffraction: float32 [16, 512, 512], P('freq'), parts along dimension 0, may hold values from -0.1875 to 0.1875
- mixing: float32 [16, 512, 512], P('freq'), parts along dimension 0, may hold values from -0.1875 to 0.1875
- coupling: float32 [512, 64, 2, 512], P('site', 'freq'), parts along dimension 1, may hold values from -1.2 to 1.2
- lists: int32 [512, 8], P('site'), may hold values from 0 to 511, as said below
- groups: int32 [512, 1], P('site'), may hold values from 0 to 31; in each aligned block of 16 rows (0 to 15, 16 to 31, ...) at most 4 rows name the same one
- jacket: float32 [32, 16, 512, 128], P('site', 'freq'), parts along dimension 1, may hold values from -0.046875 to 0.046875
Outputs:
- coefficients: float32 [512, 32, 2, 512], P('site', 'freq'), parts along dimension 1
- response: float32 [32, 32, 2, 128], P('site', 'freq'), parts along dimension 1
There are 8 independent parts, one for each index of `freq`. A program takes and returns all parts, laid end to end along the dimension named above; an argument that names none is the same for every part. Nothing has to cross between parts.
Inputs may be any that keep to these rules, and one draw needn't show every extreme that they name: No list names its own body or repeats a body; each body lists exactly 4 other bodies of its own index of site and 4 bodies of other indices; the lists of one index's bodies name exactly 2 distinct bodies of every other index of site. `groups`: among the bodies of one index of site at most 4 belong to the same group.
All inputs are finite; a program needn't handle non-finite values.
Results may differ from a plain program's by a relative error of at most 0.00012.
Values sent between devices are 32-bit elements; how exact they have to be, the bound alone decides.
A program may use at most 64 MiB of HBM per device.

v0:
```python
import jax
import jax.numpy as jnp
from jax import lax
from jax.sharding import PartitionSpec as P

CAP = 2
ITERS = 3


def complex_product(values, real_part, imag_part):
    highest = lax.Precision.HIGHEST
    first = values[..., 0, :]
    second = values[..., 1, :]
    real_out = jnp.matmul(first, real_part, precision=highest) - jnp.matmul(
        second, imag_part, precision=highest
    )
    imag_out = jnp.matmul(first, imag_part, precision=highest) + jnp.matmul(
        second, real_part, precision=highest
    )
    return jnp.stack([real_out, imag_out], axis=-2)


def phase_apply(phase, values):
    real_out = phase[..., 0, :] * values[..., 0, :] - phase[..., 1, :] * values[..., 1, :]
    imag_out = phase[..., 0, :] * values[..., 1, :] + phase[..., 1, :] * values[..., 0, :]
    return jnp.stack([real_out, imag_out], axis=-2)


def per_device(incident, diffraction, mixing, coupling, lists, groups, jacket):
    highest = lax.Precision.HIGHEST
    per_dev = incident.shape[0]
    head_count = incident.shape[1]
    mode_count = incident.shape[3]
    list_len = lists.shape[1]
    row_width = head_count * 2 * mode_count
    site_count = lax.axis_size("site")
    own_index = lax.axis_index("site")
    all_lists = lax.all_gather(lists, "site", axis=0, tiled=True)
    own_bodies = own_index * per_dev + jnp.arange(per_dev, dtype=jnp.int32)
    matches = (
        all_lists.reshape(site_count, per_dev * list_len)[:, :, None] == own_bodies[None, None, :]
    )
    other_site = jnp.arange(site_count, dtype=jnp.int32) != own_index
    wanted = jnp.any(matches, axis=1) & other_site[:, None]
    rank_send = jnp.cumsum(wanted.astype(jnp.int32), axis=1) - 1
    slot_ids = jnp.arange(CAP, dtype=jnp.int32)
    pick_table = (wanted[:, None, :] & (rank_send[:, None, :] == slot_ids[None, :, None])).astype(
        jnp.float32
    )
    pick_table = pick_table.reshape(site_count * CAP, per_dev)
    flat_lists = lists.reshape(-1)
    needed = jnp.any(
        flat_lists[:, None] == jnp.arange(site_count * per_dev, dtype=jnp.int32)[None, :], axis=0
    )
    needed = needed.reshape(site_count, per_dev)
    rank_recv = jnp.cumsum(needed.astype(jnp.int32), axis=1) - 1
    owner_dev = flat_lists // per_dev
    local_idx = flat_lists % per_dev
    slot_recv = rank_recv[owner_dev, local_idx]
    where_row = jnp.where(
        owner_dev == own_index, site_count * CAP + local_idx, owner_dev * CAP + slot_recv
    )
    coefficients = complex_product(incident, diffraction[0], diffraction[1])
    for sweep in range(ITERS):
        outgoing = complex_product(coefficients, mixing[0], mixing[1]).reshape(per_dev, row_width)
        send_rows = jnp.dot(pick_table, outgoing, precision=highest).reshape(
            site_count, CAP, row_width
        )
        arrived = lax.all_to_all(send_rows, "site", split_axis=0, concat_axis=0, tiled=True)
        row_pool = jnp.concatenate([arrived.reshape(site_count * CAP, row_width), outgoing], axis=0)
        fetched = jnp.take(row_pool, where_row, axis=0).reshape(
            per_dev, list_len, head_count, 2, mode_count
        )
        incoming = incident + jnp.sum(phase_apply(coupling[:, :, None], fetched), axis=1)
        coefficients = complex_product(incoming, diffraction[0], diffraction[1])
    flat_coef = coefficients.reshape(per_dev, row_width)
    target = groups[:, 0]
    member = (target[None, :] == jnp.arange(site_count, dtype=jnp.int32)[:, None]).astype(
        jnp.float32
    )
    group_parts = jnp.dot(member, flat_coef, precision=highest)
    own_total = lax.psum_scatter(group_parts, "site", scatter_dimension=0, tiled=True)
    group_total = own_total.reshape(1, head_count, 2, mode_count)
    response = complex_product(group_total, jacket[:, 0], jacket[:, 1])
    return (coefficients, response)


def solution(mesh):
    placed = (
        P("site", "freq", None, None),
        P("freq", None, None),
        P("freq", None, None),
        P("site", "freq", None, None),
        P("site", None),
        P("site", None),
        P("site", "freq", None, None),
    )
    return jax.shard_map(
        per_device,
        mesh=mesh,
        in_specs=placed,
        out_specs=(P("site", "freq", None, None), P("site", "freq", None, None)),
        check_vma=False,
    )
```

profile of v0, /device:TPU:8, one launch (start us, length us, event | category | flops | bytes accessed | tf_op | source)
XLA Modules:
  0.0 345.7 jit_solution(2655877701629309747)
XLA Ops:
  7.2 1.3 copy.81
  8.4 2.1 fusion.37
  10.6 2.0 fusion.50
  17.6 46.3 %all-gather = s32[32,16,8]{1,2,0:T(8,128)S(1)} all-gather(s32[1,16,8]{1,2,0:T(8,128)S(1)} %bitcast.176), channel_id=1, replica_groups=mesh['freq'=8,'site'=32] {'site'}, dimensions={0}, use_global_device_ids=true | all-gather | bytes 16896 | tf_op jit(solution)/shard_map/all_gather | solution.py:38
  65.9 1.8 copy.72
  67.7 6.6 %all-to-all-start = ((f32[32,2,4096]{2,1,0:T(2,128)}), f32[32,2,4096]{2,1,0:T(2,128)S(1)}, u32[]{:S(2)}, u32[]{:S(2)}) async-start(f32[32,2,4096]{2,1,0:T(2,128)} %copy.72), calls=%async_computation | async-start | bytes 2097152 | tf_op jit(solution)/shard_map/all_to_all | solution.py:69
  74.3 0.9 reshape.266
  75.9 1.3 gather_fusion
  77.2 1.8 fusion.123
  79.8 13.0 %all-to-all-done = f32[32,2,4096]{2,1,0:T(2,128)S(1)} async-done(((f32[32,2,4096]{2,1,0:T(2,128)}), f32[32,2,4096]{2,1,0:T(2,128)S(1)}, u32[]{:S(2)}, u32[]{:S(2)}) %all-to-all-start) | async-done | bytes 1048608 | tf_op jit(solution)/shard_map/all_to_all | solution.py:69
  92.8 1.7 reshape.267
  94.5 1.4 pad_maximum_fusion
  95.9 2.6 gather_fusion.1
  98.5 1.9 broadcast_select_fusion.2
  109.3 1.8 copy.76
  111.1 5.4 %all-to-all-start.1 = ((f32[32,2,4096]{2,1,0:T(2,128)}), f32[32,2,4096]{2,1,0:T(2,128)S(1)}, u32[]{:S(2)}, u32[]{:S(2)}) async-start(f32[32,2,4096]{2,1,0:T(2,128)} %copy.76), calls=%async_computation.1 | async-start | bytes 2097152 | tf_op jit(solution)/shard_map/all_to_all | solution.py:69
  116.5 0.9 reshape.271
  117.4 17.3 %all-to-all-done.1 = f32[32,2,4096]{2,1,0:T(2,128)S(1)} async-done(((f32[32,2,4096]{2,1,0:T(2,128)}), f32[32,2,4096]{2,1,0:T(2,128)S(1)}, u32[]{:S(2)}, u32[]{:S(2)}) %all-to-all-start.1) | async-done | bytes 1048608 | tf_op jit(solution)/shard_map/all_to_all | solution.py:69
  134.7 1.7 reshape.272
  136.4 1.4 pad_maximum_fusion.1
  137.8 2.6 gather_fusion.2
  140.4 1.9 broadcast_select_fusion.1
  151.2 1.8 copy.80
  153.0 5.6 %all-to-all-start.2 = ((f32[32,2,4096]{2,1,0:T(2,128)}), f32[32,2,4096]{2,1,0:T(2,128)S(1)}, u32[]{:S(2)}, u32[]{:S(2)}) async-start(f32[32,2,4096]{2,1,0:T(2,128)} %copy.80), calls=%async_computation.2 | async-start | bytes 2097152 | tf_op jit(solution)/shard_map/all_to_all | solution.py:69
  159.7 17.1 %all-to-all-done.2 = f32[32,2,4096]{2,1,0:T(2,128)S(1)} async-done(((f32[32,2,4096]{2,1,0:T(2,128)}), f32[32,2,4096]{2,1,0:T(2,128)S(1)}, u32[]{:S(2)}, u32[]{:S(2)}) %all-to-all-start.2) | async-done | bytes 1048608 | tf_op jit(solution)/shard_map/all_to_all | solution.py:69
  176.9 1.7 reshape.275
  178.6 1.4 pad_maximum_fusion.2
  180.0 2.6 gather_fusion.3
  182.5 1.9 broadcast_select_fusion
  189.7 1.2 fusion.99
  191.5 143.9 %all-reduce.3.cloned.1.call-done = f32[32,4096]{1,0:T(8,128)} async-done(((f32[32,4096]{1,0:T(8,128)}), f32[32,4096]{1,0:T(8,128)}) %all-reduce.3.cloned.1.call-update) | async-done | bytes 524304
  335.4 1.6 dynamic-slice_reduce_fusion
  (120 shorter events, 34.7 us)
Async XLA Ops:
  7.2 5.4 %copy-start = (f32[2,512,512]{2,1,0:T(8,128)S(1)}, f32[2,512,512]{2,1,0:T(8,128)}, u32[]{:S(2)}) copy-start(f32[2,512,512]{2,1,0:T(8,128)} %param.10) | copy-start | bytes 6291460
  8.4 4.9 %copy-start.1 = (f32[2,512,512]{2,1,0:T(8,128)S(1)}, f32[2,512,512]{2,1,0:T(8,128)}, u32[]{:S(2)}) copy-start(f32[2,512,512]{2,1,0:T(8,128)} %param.11) | copy-start | bytes 6291460
  15.6 2.0 copy-start.15
  67.7 25.2 %all-to-all-start = ((f32[32,2,4096]{2,1,0:T(2,128)}), f32[32,2,4096]{2,1,0:T(2,128)S(1)}, u32[]{:S(2)}, u32[]{:S(2)}) async-start(f32[32,2,4096]{2,1,0:T(2,128)} %copy.72), calls=%async_computation | async-start | bytes 2097152 | tf_op jit(solution)/shard_map/all_to_all | solution.py:69
  98.5 1.9 copy-start.7
  98.5 1.9 copy-start.10
  100.9 1.0 copy-start.4
  102.1 2.3 copy-start.2
  111.1 23.6 %all-to-all-start.1 = ((f32[32,2,4096]{2,1,0:T(2,128)}), f32[32,2,4096]{2,1,0:T(2,128)S(1)}, u32[]{:S(2)}, u32[]{:S(2)}) async-start(f32[32,2,4096]{2,1,0:T(2,128)} %copy.76), calls=%async_computation.1 | async-start | bytes 2097152 | tf_op jit(solution)/shard_map/all_to_all | solution.py:69
  140.4 1.9 copy-start.8
  140.4 1.9 copy-start.11
  142.8 1.0 copy-start.5
  144.0 2.3 copy-start.3
  153.0 23.9 %all-to-all-start.2 = ((f32[32,2,4096]{2,1,0:T(2,128)}), f32[32,2,4096]{2,1,0:T(2,128)S(1)}, u32[]{:S(2)}, u32[]{:S(2)}) async-start(f32[32,2,4096]{2,1,0:T(2,128)} %copy.80), calls=%async_computation.2 | async-start | bytes 2097152 | tf_op jit(solution)/shard_map/all_to_all | solution.py:69
  158.5 176.9 %all-reduce.3.cloned.1.call-start = ((), (), s32[]{:S(2)}) async-start(), calls=%async_computation.3 | async-start | bytes 1048576
  182.5 1.9 copy-start.9
  182.5 1.9 copy-start.12
  184.9 1.0 copy-start.6
  187.7 2.0 copy-start.16
  188.4 2.5 copy-start.17
  188.4 148.6 %copy-start.13 = (f32[1,2,512,128]{3,2,1,0:T(8,128)S(1)}, f32[1,2,512,128]{3,2,1,0:T(8,128)}, u32[]{:S(2)}) copy-start(f32[1,2,512,128]{3,2,1,0:T(8,128)} %param.15) | copy-start | bytes 1572868
  189.4 149.2 %copy-start.14 = (f32[16,4,2,512]{3,2,1,0:T(2,128)}, f32[16,4,2,512]{3,2,1,0:T(2,128)S(1)}, u32[]{:S(2)}) copy-start(f32[16,4,2,512]{3,2,1,0:T(2,128)S(1)} %copy.84) | copy-start | bytes 786436
Sparse Core Ops, SparseCore 0:
  191.0 144.3 all-reduce.2
where the time goes:
time: 353 us; the launch traced here: 346 us
  waiting for transfers between devices  191 us (54%)
  blocking collectives  46.3 us (13%)
  local copies, waits for them, and re-layouts  32.1 us (9%)
  matrix products  27.8 us (8%)
  starting transfers between devices  17.8 us (5%)
  other arithmetic  15.5 us (4%)
  between operations  14.8 us (4%)
    unnamed x2, waiting for transfers between devices  144 us
    all_to_all x3, waiting for transfers between devices, per_device(): lax.all_to_all(send_rows, 'site', split_axis=0, concat_axis=0, tiled=True)  47.4 us
    all_gather x1, blocking collectives, per_device(): all_lists = lax.all_gather(lists, 'site', axis=0, tiled=True)  46.3 us
    all_to_all x3, starting transfers between devices, per_device(): lax.all_to_all(send_rows, 'site', split_axis=0, concat_axis=0, tiled=True)  17.6 us
    gather x3, local copies, waits for them, and re-layouts, per_device(): jnp.take(row_pool, where_row, axis=0)  7.68 us
  transfers between devices with their start and end apart: 4, of which 4 were waited for; matrix products, arithmetic and copies ran while one was open for 2% of the time, Pallas kernels for 0%

commit v1 on v0

v1 whole, which is shorter than its diff:
```python
import jax
import jax.numpy as jnp
from jax import lax
from jax.experimental import pallas as pl
from jax.experimental.pallas import tpu as pltpu
from jax.sharding import PartitionSpec as P

ITERS = 3
NZ = 8
NX = 4
SITES = NZ * NX
BDEV = 16
K = 8
M = 512
NF = 128
ROWS = 8
POOL = 2 * SITES + BDEV
MESH = pl.DeviceIdType.MESH
F32 = jnp.float32
BF16 = jnp.bfloat16


def split(x):
    hi = x.astype(BF16)
    lo = (x - hi.astype(F32)).astype(BF16)
    return hi, lo


def turn(x):
    n = x.shape[0]
    even = lax.broadcasted_iota(jnp.int32, x.shape, 0) % 2 == 0
    return jnp.where(even, -pltpu.roll(x, n - 1, 0), pltpu.roll(x, 1, 0))


def product(x, w_hi, w_lo):
    width = w_hi.shape[1] // 2
    x_hi, x_lo = split(x)
    y = jnp.dot(x_hi, w_hi[...], preferred_element_type=F32)
    y = y + jnp.dot(x_lo, w_hi[...], preferred_element_type=F32)
    y = y + jnp.dot(x_hi, w_lo[...], preferred_element_type=F32)
    return y[:, :width] + turn(y[:, width:])


def load_matrix(src, w_hi, w_lo):
    width = src.shape[2]
    for part in range(2):
        hi, lo = split(src[part])
        w_hi[:, part * width : (part + 1) * width] = hi
        w_lo[:, part * width : (part + 1) * width] = lo


def kernel(
    incident,
    diffraction,
    mixing,
    coupling,
    lists,
    groups,
    jacket,
    coef_out,
    resp_out,
    d_hi,
    d_lo,
    m_hi,
    m_lo,
    j_hi,
    j_lo,
    lists_all,
    picks,
    places,
    picks_s,
    places_s,
    sending,
    own,
    pool_first,
    pool_second,
    pool_third,
    incoming,
    shares,
    totals,
    list_sems,
    row_send,
    row_recv,
    share_sems,
    table_sem,
):
    pools = (pool_first, pool_second, pool_third)
    me = lax.axis_index("site")
    z, x = me // NX, me % NX

    def target(slot):
        dz, dx = (slot // NX) * 5 % NZ, slot % NX
        return ((z + dz) % NZ) * NX + (x + dx) % NX

    def back(slot):
        q, dx = slot // NX, slot % NX
        return ((NZ - q) % NZ) * NX + (NX - dx) % NX

    barrier = pltpu.get_barrier_semaphore()

    @pl.loop(1, SITES)
    def _(slot):
        pl.semaphore_signal(barrier, inc=1, device_id={"site": target(slot)}, device_id_type=MESH)

    load_matrix(diffraction, d_hi, d_lo)
    load_matrix(mixing, m_hi, m_lo)
    pl.semaphore_wait(barrier, SITES - 1)

    @pl.loop(1, SITES)
    def _(slot):
        pltpu.make_async_remote_copy(
            src_ref=lists.at[0],
            dst_ref=lists_all.at[back(slot)],
            send_sem=list_sems.at[0],
            recv_sem=list_sems.at[1],
            device_id={"site": target(slot)},
            device_id_type=MESH,
        ).start()

    own_list = lists[0]
    owner = own_list // BDEV
    local = own_list % BDEV
    sites = lax.broadcasted_iota(jnp.int32, (SITES, BDEV * K), 0)
    named = owner == sites
    last = jnp.max(jnp.where(named, local, -1), axis=1, keepdims=True)
    second = jnp.max(jnp.where(named & (local == last), 1, 0), axis=0, keepdims=True)
    dz = (z - owner // NX + NZ) % NZ
    dx = (x - owner % NX + NX) % NX
    slot_of = (dz * 5 % NZ) * NX + dx
    places[...] = jnp.where(owner == me, 2 * SITES + local, 2 * slot_of + second)
    move_places = pltpu.make_async_copy(places, places_s, table_sem.at[0])
    move_places.start()
    load_matrix(jacket, j_hi, j_lo)

    coef = product(incident[...].reshape(BDEV * ROWS, M), d_hi, d_lo)
    own[...] = product(coef, m_hi, m_lo).reshape(BDEV, ROWS, M)

    pltpu.make_async_copy(lists_all.at[1:], lists_all.at[1:], list_sems.at[1]).wait()
    everyone = lists_all[:, 0, :]
    mine = everyone // BDEV == me
    wanted = everyone % BDEV
    first = jnp.min(jnp.where(mine, wanted, BDEV - 1), axis=1, keepdims=True)
    final = jnp.max(jnp.where(mine, wanted, 0), axis=1, keepdims=True)
    lane = lax.broadcasted_iota(jnp.int32, (SITES, 128), 1)
    picks[...] = jnp.where(lane == 0, first, final)
    move_picks = pltpu.make_async_copy(picks, picks_s, table_sem.at[1])
    move_picks.start()
    move_places.wait()
    move_picks.wait()

    for sweep in range(ITERS):
        pool = pools[sweep]

        @pl.loop(1, SITES)
        def _(slot):
            for row in range(2):
                sending[sweep, 2 * slot + row] = own[picks_s[slot, row]]
            pltpu.make_async_remote_copy(
                src_ref=sending.at[sweep, pl.ds(2 * slot, 2)],
                dst_ref=pool.at[pl.ds(2 * slot, 2)],
                send_sem=row_send.at[sweep],
                recv_sem=row_recv.at[sweep],
                device_id={"site": target(slot)},
                device_id_type=MESH,
            ).start()

        pool[2 * SITES :] = own[...]
        arrived = pool.at[pl.ds(2, 2 * SITES - 2)]
        pltpu.make_async_copy(arrived, arrived, row_recv.at[sweep]).wait()

        @pl.loop(0, BDEV)
        def _(body):
            straight = jnp.zeros((ROWS, M), F32)
            turned = jnp.zeros((ROWS, M), F32)
            for k in range(K):
                value = pool[places_s[0, body * K + k]]
                straight = straight + coupling[body, 2 * k : 2 * k + 1, :] * value
                turned = turned + coupling[body, 2 * k + 1 : 2 * k + 2, :] * value
            incoming[body] = incident[body] + straight + turn(turned)

        coef = product(incoming[...].reshape(BDEV * ROWS, M), d_hi, d_lo)
        if sweep < ITERS - 1:
            own[...] = product(coef, m_hi, m_lo).reshape(BDEV, ROWS, M)
    coef_out[...] = coef.reshape(BDEV, ROWS, M)

    @pl.loop(1, SITES)
    def _(slot):
        share = jnp.zeros((ROWS, M), F32)
        peer = target(slot)
        for body in range(BDEV):
            weight = jnp.where(groups[0, body] == peer, 1.0, 0.0)
            share = share + weight * coef_out[body]
        shares[slot] = share
        pltpu.make_async_remote_copy(
            src_ref=shares.at[slot],
            dst_ref=totals.at[slot],
            send_sem=share_sems.at[0],
            recv_sem=share_sems.at[1],
            device_id={"site": peer},
            device_id_type=MESH,
        ).start()

    total = jnp.zeros((ROWS, M), F32)
    for body in range(BDEV):
        weight = jnp.where(groups[0, body] == me, 1.0, 0.0)
        total = total + weight * coef_out[body]
    pltpu.make_async_copy(totals.at[1:], totals.at[1:], share_sems.at[1]).wait()
    for slot in range(1, SITES):
        total = total + totals[slot]
    resp_out[...] = product(total, j_hi, j_lo)

    pltpu.make_async_copy(lists_all.at[1:], lists_all.at[1:], list_sems.at[0]).wait()
    for sweep in range(ITERS):
        sent = sending.at[sweep, pl.ds(2, 2 * SITES - 2)]
        pltpu.make_async_copy(sent, sent, row_send.at[sweep]).wait()
    pltpu.make_async_copy(shares.at[1:], shares.at[1:], share_sems.at[0]).wait()


def per_device(incident, diffraction, mixing, coupling, lists, groups, jacket):
    vmem = pl.BlockSpec(memory_space=pltpu.VMEM)
    smem = pl.BlockSpec(memory_space=pltpu.SMEM)
    coef, resp = pl.pallas_call(
        kernel,
        out_shape=(
            jax.ShapeDtypeStruct((BDEV, ROWS, M), F32),
            jax.ShapeDtypeStruct((ROWS, NF), F32),
        ),
        in_specs=[vmem] * 5 + [smem, vmem],
        out_specs=(vmem, vmem),
        scratch_shapes=[
            pltpu.VMEM((M, 2 * M), BF16),
            pltpu.VMEM((M, 2 * M), BF16),
            pltpu.VMEM((M, 2 * M), BF16),
            pltpu.VMEM((M, 2 * M), BF16),
            pltpu.VMEM((M, 2 * NF), BF16),
            pltpu.VMEM((M, 2 * NF), BF16),
            pltpu.VMEM((SITES, 1, BDEV * K), jnp.int32),
            pltpu.VMEM((SITES, 128), jnp.int32),
            pltpu.VMEM((1, 128), jnp.int32),
            pltpu.SMEM((SITES, 128), jnp.int32),
            pltpu.SMEM((1, 128), jnp.int32),
            pltpu.VMEM((ITERS, 2 * SITES, ROWS, M), F32),
            pltpu.VMEM((BDEV, ROWS, M), F32),
            pltpu.VMEM((POOL, ROWS, M), F32),
            pltpu.VMEM((POOL, ROWS, M), F32),
            pltpu.VMEM((POOL, ROWS, M), F32),
            pltpu.VMEM((BDEV, ROWS, M), F32),
            pltpu.VMEM((SITES, ROWS, M), F32),
            pltpu.VMEM((SITES, ROWS, M), F32),
            pltpu.SemaphoreType.DMA((2,)),
            pltpu.SemaphoreType.DMA((ITERS,)),
            pltpu.SemaphoreType.DMA((ITERS,)),
            pltpu.SemaphoreType.DMA((2,)),
            pltpu.SemaphoreType.DMA((2,)),
        ],
        compiler_params=pltpu.CompilerParams(
            collective_id=0, has_side_effects=True, vmem_limit_bytes=48 * 1024 * 1024
        ),
        cost_estimate=pl.CostEstimate(
            flops=3_000_000_000, bytes_accessed=6_000_000, transcendentals=0
        ),
    )(
        incident.reshape(BDEV, ROWS, M),
        diffraction,
        mixing,
        coupling.reshape(BDEV, 2 * K, M),
        lists.reshape(1, 1, BDEV * K),
        groups.reshape(1, BDEV),
        jacket.reshape(2, M, NF),
    )
    return coef.reshape(BDEV, 4, 2, M), resp.reshape(1, 4, 2, NF)


def solution(mesh):
    placed = (
        P("site", "freq", None, None),
        P("freq", None, None),
        P("freq", None, None),
        P("site", "freq", None, None),
        P("site", None),
        P("site", None),
        P("site", "freq", None, None),
    )
    return jax.shard_map(
        per_device,
        mesh=mesh,
        in_specs=placed,
        out_specs=(P("site", "freq", None, None), P("site", "freq", None, None)),
        check_vma=False,
    )
```

time: 353 us -> 119 us (0.34); the launches traced: 346 us -> 119 us
  waiting for transfers between devices: 191 us -> 0 us
  Pallas kernels: 0 us -> 109 us
  blocking collectives: 46.3 us -> 0 us
  matrix products: 27.8 us -> 0 us
  local copies, waits for them, and re-layouts: 32.1 us -> 9.7 us
  starting transfers between devices: 17.8 us -> 0 us
  other arithmetic: 15.5 us -> 0 us
  between operations: 14.8 us -> 0.66 us
    unnamed x2 -> x0, waiting for transfers between devices: 144 us -> none
    pallas_call x0 -> x1, Pallas kernels: none -> 109 us  [per_device(): pl.pallas_call(kernel, out_shape=(jax.ShapeDtypeStruct((BDEV, ROWS, M), F...]
    all_to_all x3 -> x0, waiting for transfers between devices: 47.4 us -> none  [per_device(): lax.all_to_all(send_rows, 'site', split_axis=0, concat_axis=0, tiled=True)]
    all_gather x1 -> x0, blocking collectives: 46.3 us -> none  [per_device(): all_lists = lax.all_gather(lists, 'site', axis=0, tiled=True)]
    dot_general x36 -> x0, matrix products: 27.8 us -> none  [the longest x8 6.91 us: complex_product(): jnp.matmul(first, imag_part, precision=highest)]
    all_to_all x3 -> x0, starting transfers between devices: 17.6 us -> none  [per_device(): lax.all_to_all(send_rows, 'site', split_axis=0, concat_axis=0, tiled=True)]
    gather x4 -> x0, local copies, waits for them, and re-layouts: 8.95 us -> none  [the longest x3 7.68 us: per_device(): jnp.take(row_pool, where_row, axis=0)]
    select_n x3 -> x0, other arithmetic: 5.69 us -> none  [per_device(): jnp.take(row_pool, where_row, axis=0)]
  transfers between devices with their start and end apart: 4 -> 0, of which waited for: 4 -> 0; matrix products, arithmetic and copies ran while one was open for 2% -> 0% of each run, Pallas kernels for 0% -> 0%
where the time goes in v1:
time: 119 us
  Pallas kernels  109 us (92%)
  local copies, waits for them, and re-layouts  9.7 us (8%)
    pallas_call x1, Pallas kernels, per_device(): pl.pallas_call(kernel, out_shape=(jax.ShapeDtypeStruct((BDEV, ROWS, M), F...  109 us
    unnamed x10, local copies, waits for them, and re-layouts  6.22 us

profile of v1, /device:TPU:8, one launch (start us, length us, event | category | flops | bytes accessed | tf_op | source)
XLA Modules:
  0.0 118.9 jit_solution(4389523752790761317)
XLA Ops:
  0.6 0.8 copy.10
  1.4 0.1 reshape.27.lists
  1.5 1.1 reshape.25.incident
  2.6 1.4 %reshape.26.coupling = f32[16,16,512]{2,1,0:T(8,128)S(1)} reshape(f32[16,8,2,512]{3,2,1,0:T(2,128)} %param.10) | data formatting | bytes 1048576 | tf_op jit(solution)/shard_map/reshape | solution.py:266
  4.0 0.0 copy-start
  4.0 1.6 %copy-done = f32[2,512,512]{2,1,0:T(8,128)S(1)} copy-done((f32[2,512,512]{2,1,0:T(8,128)S(1)}, f32[2,512,512]{2,1,0:T(8,128)}, u32[]{:S(2)}) %copy-start) | copy-done | bytes 2097176
  5.6 0.0 copy-start.1
  5.6 1.6 %copy-done.1 = f32[2,512,512]{2,1,0:T(8,128)S(1)} copy-done((f32[2,512,512]{2,1,0:T(8,128)S(1)}, f32[2,512,512]{2,1,0:T(8,128)}, u32[]{:S(2)}) %copy-start.1) | copy-done | bytes 2097176
  7.2 0.0 copy-start.2
  7.2 1.0 copy-done.2
  8.2 0.0 copy-start.3
  8.3 0.7 copy-done.3
  8.9 108.6 %shard_map.86 = (f32[16,8,512]{2,1,0:T(8,128)S(1)}, f32[8,128]{1,0:T(8,128)S(1)}) custom-call(f32[16,8,512]{2,1,0:T(8,128)S(1)} %reshape.25.incident, f32[2,512,512]{2,1,0:T(8,128)S(1)} %copy-done, f32[2,512,512]{2,1,0:T(8,128)S(1)} %copy-done.1, f32[16,16,512]{2,1,0:T(8,128)S(1)} %reshape.26.coupling, s32[1,1,128]{2,1,0:T(1,128)S(1)} %reshape.27.lists, ...), custom_call_target="tpu_custom_call" | custom-call | flops 3000000000 | bytes 6000000 | tf_op jit(solution)/shard_map/pallas_call | solution.py:222
  117.5 0.8 reshape.30
  118.3 0.6 copy.12
Async XLA Ops:
  4.0 1.6 %copy-start = (f32[2,512,512]{2,1,0:T(8,128)S(1)}, f32[2,512,512]{2,1,0:T(8,128)}, u32[]{:S(2)}) copy-start(f32[2,512,512]{2,1,0:T(8,128)} %diffraction.1) | copy-start | bytes 6291460
  5.6 1.6 %copy-start.1 = (f32[2,512,512]{2,1,0:T(8,128)S(1)}, f32[2,512,512]{2,1,0:T(8,128)}, u32[]{:S(2)}) copy-start(f32[2,512,512]{2,1,0:T(8,128)} %mixing.1) | copy-start | bytes 6291460
  7.2 1.0 copy-start.2
  8.2 0.7 copy-start.3

commit v2 on v0

v2 whole, which is shorter than its diff:
```python
import jax
import jax.numpy as jnp
from jax import lax
from jax.experimental import pallas as pl
from jax.experimental.pallas import tpu as pltpu
from jax.sharding import PartitionSpec as P

ITERS = 3
NZ = 8
NX = 4
SITES = NZ * NX
BDEV = 16
K = 8
M = 512
HALF = M // 2
NF = 128
ROWS = 8
TEAMS = 2
POOL = 2 * SITES + BDEV
LOCAL = 6
MESH = pl.DeviceIdType.MESH
F32 = jnp.float32
BF16 = jnp.bfloat16


def split(x):
    hi = x.astype(BF16)
    lo = (x - hi.astype(F32)).astype(BF16)
    return hi, lo


def turn(x):
    n = x.shape[0]
    even = lax.broadcasted_iota(jnp.int32, x.shape, 0) % 2 == 0
    return jnp.where(even, -pltpu.roll(x, n - 1, 0), pltpu.roll(x, 1, 0))


def product(x, w_hi, w_lo):
    rows, width = x.shape[0], w_hi.shape[1] // 2
    x_hi, x_lo = split(x)
    y = jnp.dot(jnp.concatenate([x_hi, x_lo], axis=0), w_hi[...], preferred_element_type=F32)
    y = y[:rows] + y[rows:] + jnp.dot(x_hi, w_lo[...], preferred_element_type=F32)
    return y[:, :width] + turn(y[:, width:])


def load_matrix(src, w_hi, w_lo):
    width = src.shape[2]
    for part in range(2):
        hi, lo = split(src[part])
        w_hi[:, part * width : (part + 1) * width] = hi
        w_lo[:, part * width : (part + 1) * width] = lo


def swap_halves(a, b):
    upper = lax.broadcasted_iota(jnp.int32, a.shape, 1) < ROWS // 2
    first = jnp.where(upper, a, pltpu.roll(b, ROWS // 2, 1))
    second = jnp.where(upper, pltpu.roll(a, ROWS // 2, 1), b)
    return first, second


def to_rows(tiles):
    pairs = tiles.reshape(BDEV // 2, 2, ROWS, HALF)
    low, high = swap_halves(pairs[:, 0], pairs[:, 1])
    return jnp.concatenate([low, high], axis=-1).reshape(BDEV * ROWS // 2, M)


def store_tiles(out, rows):
    rows = rows.reshape(BDEV // 2, ROWS, M)
    even, odd = swap_halves(rows[:, :, :HALF], rows[:, :, HALF:])
    for pair in range(BDEV // 2):
        out[2 * pair] = even[pair]
        out[2 * pair + 1] = odd[pair]


def kernel(*refs):
    refs = list(refs)

    def take(count):
        taken = refs[:count]
        del refs[:count]
        return taken

    incident_h, diffraction_h, mixing_h, coupling_h, lists, groups, jacket_h = take(7)
    coef_out, resp_out = take(2)
    incident_v, diffraction_v, mixing_v, coupling_v, jacket_v = take(5)
    d_hi, d_lo, m_hi, m_lo, j_hi, j_lo = take(6)
    incident, factor, incoming, result, own = take(5)
    lists_all, picks, places, picks_s, places_s = take(5)
    sending, shares, totals = take(3)
    pools = [take(TEAMS) for _ in range(ITERS)]
    relays = [[take(2) for _ in range(TEAMS)] for _ in range(ITERS)]
    in_sems, list_sems, dense_send, dense_recv, row_send, row_recv, share_send, share_recv, table_sem = take(9)

    me = lax.axis_index("site")
    z, x = me // NX, me % NX

    def at(dz, dx):
        return ((z + dz + NZ) % NZ) * NX + (x + dx) % NX

    def send(src, dst, send_sem, recv_sem, site):
        pltpu.make_async_remote_copy(
            src_ref=src,
            dst_ref=dst,
            send_sem=send_sem,
            recv_sem=recv_sem,
            device_id={"site": site},
            device_id_type=MESH,
        ).start()

    def done(ref, sem):
        pltpu.make_async_copy(ref, ref, sem).wait()

    def place_of(behind, aside):
        return aside * NZ + (behind + 1) % NZ

    loads = [
        pltpu.make_async_copy(src, dst, in_sems.at[i])
        for i, (src, dst) in enumerate(
            (
                (incident_h, incident_v),
                (diffraction_h, diffraction_v),
                (mixing_h, mixing_v),
                (coupling_h, coupling_v),
                (jacket_h, jacket_v),
            )
        )
    ]
    for load in loads:
        load.start()

    barrier = pltpu.get_barrier_semaphore()

    @pl.loop(1, SITES)
    def _(step):
        site = at(step // NX, step % NX)
        pl.semaphore_signal(barrier, inc=1, device_id={"site": site}, device_id_type=MESH)

    loads[0].wait()
    heads = incident_v[...]
    first, second = swap_halves(heads[:, :, :HALF], heads[:, :, HALF:])
    incident[0] = first
    incident[1] = second
    loads[1].wait()
    load_matrix(diffraction_v, d_hi, d_lo)
    loads[2].wait()
    load_matrix(mixing_v, m_hi, m_lo)

    def outgoing_of(sweep, team, tiles):
        coef = product(to_rows(tiles), d_hi, d_lo)
        store_tiles(own.at[sweep, team], product(coef, m_hi, m_lo))

    for team in range(TEAMS):
        outgoing_of(0, team, incident[team])

    own_list = lists[0]
    owner = own_list // BDEV
    local = own_list % BDEV
    sites = lax.broadcasted_iota(jnp.int32, (SITES, BDEV * K), 0)
    named = owner == sites
    last = jnp.max(jnp.where(named, local, -1), axis=1, keepdims=True)
    later = jnp.max(jnp.where(named & (local == last), 1, 0), axis=0, keepdims=True)
    behind = (z - owner // NX + NZ) % NZ
    aside = (x - owner % NX + NX) % NX
    places[...] = jnp.where(owner == me, 2 * SITES + local, 2 * place_of(behind, aside) + later)
    move_places = pltpu.make_async_copy(places, places_s, table_sem.at[0])
    move_places.start()
    lists_all[0] = lists[0]

    loads[3].wait()
    tile_upper = lax.broadcasted_iota(jnp.int32, (ROWS, HALF), 0) < ROWS // 2

    @pl.loop(0, BDEV)
    def _(body):
        for k in range(2 * K):
            factor[body, k] = jnp.where(
                tile_upper,
                coupling_v[body, k : k + 1, :HALF],
                coupling_v[body, k : k + 1, HALF:],
            )

    loads[4].wait()
    load_matrix(jacket_v, j_hi, j_lo)

    pl.semaphore_wait(barrier, SITES - 1)

    def send_dense(sweep, team):
        for way, step in enumerate((1, -1)):
            send(
                own.at[sweep, team],
                relays[sweep][team][way],
                dense_send.at[sweep, team],
                dense_recv.at[sweep, team, way],
                at(step, 0),
            )

    def send_aside(sweep, team):
        for dx in range(1, NX):
            row = 2 * place_of(0, dx)
            for i in range(2):
                sending[sweep, team, row + i] = own[sweep, team, picks_s[dx, i]]
            send(
                sending.at[sweep, team, pl.ds(row, 2)],
                pools[sweep][team].at[pl.ds(row, 2)],
                row_send.at[sweep, team],
                row_recv.at[sweep, team],
                at(0, dx),
            )

    def pass_on(sweep, team):
        pool = pools[sweep][team]
        for way in range(2):
            done(relays[sweep][team][way], dense_recv.at[sweep, team, way])

        def forward(way, hop, dx, number, skip):
            step = (1, -1)[way]
            block = relays[sweep][team][way]
            row = 2 * place_of((step * (hop + 1) + NZ) % NZ, dx) + skip
            entry = ((step * hop + NZ) % NZ) * NX + dx
            for i in range(number):
                sending[sweep, team, row + i] = block[picks_s[entry, 2 + 2 * way + skip + i]]
            send(
                sending.at[sweep, team, pl.ds(row, number)],
                pool.at[pl.ds(row, number)],
                row_send.at[sweep, team],
                row_recv.at[sweep, team],
                at(step * hop, dx),
            )

        @pl.loop(0, NX)
        def _(dx):
            for way in range(2):
                forward(way, NZ // 2 - 1, dx, 1, way)

        @pl.loop(0, 3 * NX - 1)
        def _(i):
            item = 3 * NX - 1 - i
            for way in range(2):
                forward(way, item // NX, item % NX, 2, 0)

        pool[2 * SITES :] = own[sweep, team]
        for way in range(2):
            row = 2 * place_of((1, NZ - 1)[way], 0)
            for i in range(2):
                pool[row + i] = relays[sweep][team][way][picks_s[0, 2 + 2 * way + i]]

    def gather(sweep, team):
        pool = pools[sweep][team]
        done(pool.at[pl.ds(LOCAL, 2 * SITES - LOCAL)], row_recv.at[sweep, team])

        @pl.loop(0, BDEV)
        def _(body):
            straight = incident[team, body]
            turned = jnp.zeros((ROWS, HALF), F32)
            for k in range(K):
                value = pool[places_s[0, body * K + k]]
                straight = straight + factor[body, 2 * k] * value
                turned = turned + factor[body, 2 * k + 1] * value
            incoming[team, body] = straight + turn(turned)

    def share_of(team, site):
        share = jnp.zeros((ROWS, HALF), F32)
        for body in range(BDEV):
            share = share + jnp.where(groups[0, body] == site, 1.0, 0.0) * incoming[team, body]
        return share

    def send_shares(team):
        @pl.loop(1, SITES)
        def _(step):
            site = at(step // NX, step % NX)
            shares[team, step] = share_of(team, site)
            send(
                shares.at[team, step],
                totals.at[team, step],
                share_send.at[team],
                share_recv.at[team],
                site,
            )

    @pl.loop(1, SITES)
    def _(step):
        dz, dx = step // NX, step % NX
        send(
            lists.at[0],
            lists_all.at[((NZ - dz) % NZ) * NX + (NX - dx) % NX],
            list_sems.at[0],
            list_sems.at[1],
            at(dz, dx),
        )

    for team in range(TEAMS):
        send_dense(0, team)

    done(lists_all.at[1:], list_sems.at[1])
    everyone = lists_all[:, 0, :]
    lane = lax.broadcasted_iota(jnp.int32, (SITES, 128), 1)
    table = jnp.zeros((SITES, 128), jnp.int32)
    for i, source in enumerate((me, at(-1, 0), at(1, 0))):
        theirs = everyone // BDEV == source
        wanted = everyone % BDEV
        smallest = jnp.min(jnp.where(theirs, wanted, BDEV - 1), axis=1, keepdims=True)
        largest = jnp.max(jnp.where(theirs, wanted, 0), axis=1, keepdims=True)
        table = jnp.where(lane == 2 * i, smallest, table)
        table = jnp.where(lane == 2 * i + 1, largest, table)
    picks[...] = table
    move_picks = pltpu.make_async_copy(picks, picks_s, table_sem.at[1])
    move_picks.start()
    move_places.wait()
    move_picks.wait()

    for sweep in range(ITERS):
        if sweep == 0:
            for team in range(TEAMS):
                send_aside(sweep, team)
        for team in range(TEAMS):
            pass_on(sweep, team)
        if sweep < ITERS - 1:
            for team in range(TEAMS):
                gather(sweep, team)
                outgoing_of(sweep + 1, team, incoming[team])
                send_dense(sweep + 1, team)
                send_aside(sweep + 1, team)

    for team in range(TEAMS):
        gather(ITERS - 1, team)
        send_shares(team)
        store_tiles(result.at[team], product(to_rows(incoming[team]), d_hi, d_lo))
    low, high = swap_halves(result[0], result[1])
    coef_out[:, :, :HALF] = low
    coef_out[:, :, HALF:] = high

    sums = []
    for team in range(TEAMS):
        total = share_of(team, me)
        done(totals.at[team, pl.ds(1, SITES - 1)], share_recv.at[team])
        for step in range(1, SITES):
            total = total + totals[team, step]
        sums.append(total[None])
    low, high = swap_halves(sums[0], sums[1])
    total = jnp.concatenate([low[0], high[0]], axis=-1)
    resp_out[...] = product(product(total, d_hi, d_lo), j_hi, j_lo)

    done(lists_all.at[1:], list_sems.at[0])
    for team in range(TEAMS):
        for sweep in range(ITERS):
            for _ in range(2):
                done(own.at[sweep, team], dense_send.at[sweep, team])
            done(sending.at[sweep, team, pl.ds(LOCAL, 2 * SITES - LOCAL)], row_send.at[sweep, team])
        done(shares.at[team, pl.ds(1, SITES - 1)], share_send.at[team])


def per_device(incident, diffraction, mixing, coupling, lists, groups, jacket):
    vmem = pl.BlockSpec(memory_space=pltpu.VMEM)
    smem = pl.BlockSpec(memory_space=pltpu.SMEM)
    anywhere = pl.BlockSpec(memory_space=pl.ANY)

    def f32(*shape):
        return pltpu.VMEM(shape, F32)

    def dma(*shape):
        return pltpu.SemaphoreType.DMA(shape)

    coef, resp = pl.pallas_call(
        kernel,
        out_shape=(
            jax.ShapeDtypeStruct((BDEV, ROWS, M), F32),
            jax.ShapeDtypeStruct((ROWS, NF), F32),
        ),
        in_specs=[anywhere] * 4 + [vmem, smem, anywhere],
        out_specs=(vmem, vmem),
        scratch_shapes=[
            f32(BDEV, ROWS, M),
            f32(2, M, M),
            f32(2, M, M),
            f32(BDEV, 2 * K, M),
            f32(2, M, NF),
            *[pltpu.VMEM((M, 2 * M), BF16)] * 4,
            *[pltpu.VMEM((M, 2 * NF), BF16)] * 2,
            f32(TEAMS, BDEV, ROWS, HALF),
            f32(BDEV, 2 * K, ROWS, HALF),
            f32(TEAMS, BDEV, ROWS, HALF),
            f32(TEAMS, BDEV, ROWS, HALF),
            f32(ITERS, TEAMS, BDEV, ROWS, HALF),
            pltpu.VMEM((SITES, 1, BDEV * K), jnp.int32),
            pltpu.VMEM((SITES, 128), jnp.int32),
            pltpu.VMEM((1, 128), jnp.int32),
            pltpu.SMEM((SITES, 128), jnp.int32),
            pltpu.SMEM((1, 128), jnp.int32),
            f32(ITERS, TEAMS, 2 * SITES, ROWS, HALF),
            f32(TEAMS, SITES, ROWS, HALF),
            f32(TEAMS, SITES, ROWS, HALF),
            *[f32(POOL, ROWS, HALF)] * (ITERS * TEAMS),
            *[f32(BDEV, ROWS, HALF)] * (ITERS * TEAMS * 2),
            dma(5),
            dma(2),
            dma(ITERS, TEAMS),
            dma(ITERS, TEAMS, 2),
            dma(ITERS, TEAMS),
            dma(ITERS, TEAMS),
            dma(TEAMS),
            dma(TEAMS),
            dma(2),
        ],
        compiler_params=pltpu.CompilerParams(
            collective_id=0, has_side_effects=True, vmem_limit_bytes=52 * 1024 * 1024
        ),
        cost_estimate=pl.CostEstimate(
            flops=3_000_000_000, bytes_accessed=6_000_000, transcendentals=0
        ),
    )(
        incident.reshape(BDEV, ROWS, M),
        diffraction,
        mixing,
        coupling.reshape(BDEV, 2 * K, M),
        lists.reshape(1, 1, BDEV * K),
        groups.reshape(1, BDEV),
        jacket.reshape(2, M, NF),
    )
    return coef.reshape(BDEV, 4, 2, M), resp.reshape(1, 4, 2, NF)


def solution(mesh):
    placed = (
        P("site", "freq", None, None),
        P("freq", None, None),
        P("freq", None, None),
        P("site", "freq", None, None),
        P("site", None),
        P("site", None),
        P("site", "freq", None, None),
    )
    return jax.shard_map(
        per_device,
        mesh=mesh,
        in_specs=placed,
        out_specs=(P("site", "freq", None, None), P("site", "freq", None, None)),
        check_vma=False,
    )
```

time: 353 us -> 91.3 us (0.26); the launches traced: 346 us -> 90.5 us
  waiting for transfers between devices: 191 us -> 0 us
  Pallas kernels: 0 us -> 83.4 us
  blocking collectives: 46.3 us -> 0 us
  matrix products: 27.8 us -> 0 us
  local copies, waits for them, and re-layouts: 32.1 us -> 6.52 us
  starting transfers between devices: 17.8 us -> 0 us
  other arithmetic: 15.5 us -> 0 us
  between operations: 14.8 us -> 0.66 us
    unnamed x2 -> x0, waiting for transfers between devices: 144 us -> none
    pallas_call x0 -> x1, Pallas kernels: none -> 83.4 us  [per_device(): pl.pallas_call(kernel, out_shape=(jax.ShapeDtypeStruct((BDEV, ROWS, M), F...]
    all_to_all x3 -> x0, waiting for transfers between devices: 47.4 us -> none  [per_device(): lax.all_to_all(send_rows, 'site', split_axis=0, concat_axis=0, tiled=True)]
    all_gather x1 -> x0, blocking collectives: 46.3 us -> none  [per_device(): all_lists = lax.all_gather(lists, 'site', axis=0, tiled=True)]
    dot_general x36 -> x0, matrix products: 27.8 us -> none  [the longest x8 6.91 us: complex_product(): jnp.matmul(first, imag_part, precision=highest)]
    all_to_all x3 -> x0, starting transfers between devices: 17.6 us -> none  [per_device(): lax.all_to_all(send_rows, 'site', split_axis=0, concat_axis=0, tiled=True)]
    gather x4 -> x0, local copies, waits for them, and re-layouts: 8.95 us -> none  [the longest x3 7.68 us: per_device(): jnp.take(row_pool, where_row, axis=0)]
    select_n x3 -> x0, other arithmetic: 5.69 us -> none  [per_device(): jnp.take(row_pool, where_row, axis=0)]
  transfers between devices with their start and end apart: 4 -> 0, of which waited for: 4 -> 0; matrix products, arithmetic and copies ran while one was open for 2% -> 0% of each run, Pallas kernels for 0% -> 0%
where the time goes in v2:
time: 91.3 us; the launch traced here: 90.5 us
  Pallas kernels  83.4 us (91%)
  local copies, waits for them, and re-layouts  6.52 us (7%)
    pallas_call x1, Pallas kernels, per_device(): pl.pallas_call(kernel, out_shape=(jax.ShapeDtypeStruct((BDEV, ROWS, M), F...  83.4 us
    unnamed x6, local copies, waits for them, and re-layouts  3.04 us

profile of v2, /device:TPU:8, one launch (start us, length us, event | category | flops | bytes accessed | tf_op | source)
XLA Modules:
  0.0 90.5 jit_solution(8778247108714140486)
XLA Ops:
  0.6 0.8 copy.10
  1.4 0.1 reshape.27.refs_4_
  1.5 1.1 %reshape.25.refs_0_ = f32[16,8,512]{2,1,0:T(8,128)S(1)} reshape(f32[16,4,2,512]{3,2,1,0:T(2,128)} %param.7) | data formatting | bytes 524288 | tf_op jit(solution)/shard_map/reshape | solution.py:410
  2.6 1.4 %reshape.26.refs_3_ = f32[16,16,512]{2,1,0:T(8,128)S(1)} reshape(f32[16,8,2,512]{3,2,1,0:T(2,128)} %param.10) | data formatting | bytes 1048576 | tf_op jit(solution)/shard_map/reshape | solution.py:413
  4.0 0.0 copy-start
  4.0 1.0 %copy-done = f32[1,2,512,128]{3,2,1,0:T(8,128)S(1)} copy-done((f32[1,2,512,128]{3,2,1,0:T(8,128)S(1)}, f32[1,2,512,128]{3,2,1,0:T(8,128)}, u32[]{:S(2)}) %copy-start) | copy-done | bytes 524312
  5.1 0.0 copy-start.1
  5.1 0.7 copy-done.1
  5.7 83.4 %shard_map.86 = (f32[16,8,512]{2,1,0:T(8,128)S(1)}, f32[8,128]{1,0:T(8,128)S(1)}) custom-call(f32[16,8,512]{2,1,0:T(8,128)S(1)} %reshape.25.refs_0_, f32[2,512,512]{2,1,0:T(8,128)} %refs_1_.1, f32[2,512,512]{2,1,0:T(8,128)} %refs_2_.1, f32[16,16,512]{2,1,0:T(8,128)S(1)} %reshape.26.refs_3_, s32[1,1,128]{2,1,0:T(1,128)S(1)} %reshape.27.refs_4_, ...), custom_call_target="tpu_custom_call" | custom-call | flops 3000000000 | bytes 6000000 | tf_op jit(solution)/shard_map/pallas_call | solution.py:362
  89.1 0.8 reshape.30
  90.0 0.6 copy.12
Async XLA Ops:
  4.0 1.0 %copy-start = (f32[1,2,512,128]{3,2,1,0:T(8,128)S(1)}, f32[1,2,512,128]{3,2,1,0:T(8,128)}, u32[]{:S(2)}) copy-start(f32[1,2,512,128]{3,2,1,0:T(8,128)} %param.13) | copy-start | bytes 1572868
  5.1 0.7 copy-start.1

commit v3 on v2

v3 whole, which is shorter than its diff:
```python
import jax
import jax.numpy as jnp
from jax import lax
from jax.experimental import pallas as pl
from jax.experimental.pallas import tpu as pltpu
from jax.sharding import PartitionSpec as P

ITERS = 3
NZ = 8
NX = 4
SITES = NZ * NX
BDEV = 16
K = 8
M = 512
LANES = 128
QUADS = M // LANES
NF = 128
ROWS = 8
TEAMS = 4
POOL = 2 * SITES + BDEV
LOCAL = 10
WAYS = (1, -1)
MESH = pl.DeviceIdType.MESH
F32 = jnp.float32
BF16 = jnp.bfloat16


def split(x):
    hi = x.astype(BF16)
    lo = (x - hi.astype(F32)).astype(BF16)
    return hi, lo


def is_real(shape):
    return lax.broadcasted_iota(jnp.int32, shape, 0) % 2 == 0


def turn(x):
    n = x.shape[0]
    return jnp.where(is_real(x.shape), -pltpu.roll(x, n - 1, 0), pltpu.roll(x, 1, 0))


def product(x, w_hi, w_lo):
    rows, width = x.shape[0], w_hi.shape[1] // 2
    x_hi, x_lo = split(x)
    y = jnp.dot(jnp.concatenate([x_hi, x_lo], axis=0), w_hi[...], preferred_element_type=F32)
    y = y[:rows] + y[rows:] + jnp.dot(x_hi, w_lo[...], preferred_element_type=F32)
    return y[:, :width] + turn(y[:, width:])


def load_matrix(src, w_hi, w_lo):
    width = src.shape[2]
    for part in range(2):
        hi, lo = split(src[part])
        w_hi[:, part * width : (part + 1) * width] = hi
        w_lo[:, part * width : (part + 1) * width] = lo


def exchange(a, b, span):
    even = lax.broadcasted_iota(jnp.int32, a.shape, 1) // span % 2 == 0
    first = jnp.where(even, a, pltpu.roll(b, span, 1))
    second = jnp.where(even, pltpu.roll(a, ROWS - span, 1), b)
    return first, second


def transpose_quads(tiles):
    t0, t2 = exchange(tiles[0], tiles[2], 4)
    t1, t3 = exchange(tiles[1], tiles[3], 4)
    return (*exchange(t0, t1, 2), *exchange(t2, t3, 2))


def to_rows(tiles):
    count = tiles.shape[0]
    fours = tiles.reshape(count // 4, 4, ROWS, LANES)
    blocks = transpose_quads([fours[:, i] for i in range(4)])
    return jnp.concatenate(blocks, axis=-1).reshape(count * 2, M)


def to_tiles(rows):
    stacked = rows.reshape(rows.shape[0] // ROWS, ROWS, M)
    blocks = [stacked[:, :, q * LANES : (q + 1) * LANES] for q in range(QUADS)]
    fours = transpose_quads(blocks)
    return [fours[body % 4][body // 4] for body in range(rows.shape[0] // 2)]


def kernel(*refs):
    refs = list(refs)

    def take(count):
        taken = refs[:count]
        del refs[:count]
        return taken

    incident_h, diffraction_h, mixing_h, coupling_h, lists_h, groups_h, jacket_h = take(7)
    coef_out, resp_out = take(2)
    incident, diffraction_v, mixing_v, coupling_v, jacket_v, lists, groups = take(7)
    d_hi, d_lo, m_hi, m_lo, j_hi, j_lo = take(6)
    factor, incoming, own = take(3)
    lists_all, picks, places, named_by, member, picks_s, places_s = take(7)
    sending, shares, aside_parts, totals = take(4)
    pools = [take(TEAMS) for _ in range(ITERS)]
    near = [[take(2) for _ in range(TEAMS)] for _ in range(ITERS)]
    far = [[take(2) for _ in range(TEAMS)] for _ in range(ITERS)]
    in_sems, list_sems, dense_send, near_recv, far_recv, row_send, row_recv, part_sems, share_sems, table_sem = take(10)

    me = lax.axis_index("site")
    z, x = me // NX, me % NX

    z_parts = [(z + dz) % NZ * NX for dz in range(NZ)]
    x_parts = [(x + dx) % NX for dx in range(NX)]

    def at(dz, dx):
        return z_parts[dz % NZ] + x_parts[dx % NX]

    def send(src, dst, send_sem, recv_sem, site):
        pltpu.make_async_remote_copy(
            src_ref=src,
            dst_ref=dst,
            send_sem=send_sem,
            recv_sem=recv_sem,
            device_id={"site": site},
            device_id_type=MESH,
        ).start()

    def done(ref, sem):
        pltpu.make_async_copy(ref, ref, sem).wait()

    def place_of(behind, aside):
        return aside * NZ + (behind + 2) % NZ

    def outgoing_of(sweep, team, tiles):
        coef = product(to_rows(tiles), d_hi, d_lo)
        for body, tile in enumerate(to_tiles(product(coef, m_hi, m_lo))):
            own[sweep, team, body] = tile

    def send_dense(sweep, team):
        for way, step in enumerate(WAYS):
            send(
                own.at[sweep, team],
                near[sweep][team][way],
                dense_send.at[sweep, team],
                near_recv.at[sweep, team, way],
                at(step, 0),
            )

    def send_picked(sweep, team, block, dz, dx, behind, lane, number, skip):
        row = 2 * place_of((behind + NZ) % NZ, dx) + skip
        entry = ((dz + NZ) % NZ) * NX + dx
        for i in range(number):
            sending[sweep, team, row + i] = block[picks_s[entry, lane + skip + i]]
        send(
            sending.at[sweep, team, pl.ds(row, number)],
            pools[sweep][team].at[pl.ds(row, number)],
            row_send.at[sweep, team],
            row_recv.at[sweep, team],
            at(dz, dx),
        )

    def send_aside(sweep, team):
        for dx in range(1, NX):
            send_picked(sweep, team, own.at[sweep, team], 0, dx, 0, 0, 2, 0)

    def pass_near(sweep, team):
        for way, step in enumerate(WAYS):
            done(near[sweep][team][way], near_recv.at[sweep, team, way])
            send(
                near[sweep][team][way],
                far[sweep][team][way],
                dense_send.at[sweep, team],
                far_recv.at[sweep, team, way],
                at(step, 0),
            )

        for dx in range(1, NX):
            for way, step in enumerate(WAYS):
                send_picked(sweep, team, near[sweep][team][way], 0, dx, step, 2 + 2 * way, 2, 0)

    def pass_far(sweep, team):
        for way in range(2):
            done(far[sweep][team][way], far_recv.at[sweep, team, way])

        for dx in range(NX):
            for way, step in enumerate(WAYS):
                send_picked(sweep, team, far[sweep][team][way], 2 * step, dx, 4 * step, 6 + 2 * way, 1, way)

        for item in range(2 * NX - 1, 0, -1):
            hop, dx = item // NX, item % NX
            for way, step in enumerate(WAYS):
                send_picked(
                    sweep, team, far[sweep][team][way], step * hop, dx, step * (hop + 2), 6 + 2 * way, 2, 0
                )

        pool = pools[sweep][team]
        pool[2 * SITES :] = own[sweep, team]
        for way, step in enumerate(WAYS):
            for distance, blocks in ((1, near), (2, far)):
                row = 2 * place_of((step * distance + NZ) % NZ, 0)
                for i in range(2):
                    pool[row + i] = blocks[sweep][team][way][picks_s[0, 4 * distance - 2 + 2 * way + i]]

    def gather(sweep, team):
        pool = pools[sweep][team]
        done(pool.at[pl.ds(LOCAL, 2 * SITES - LOCAL)], row_recv.at[sweep, team])

        @pl.loop(0, BDEV // 4)
        def _(four):
            for i in range(4):
                body = 4 * four + i
                straight = incident[body, team]
                turned = jnp.zeros((ROWS, LANES), F32)
                for k in range(K):
                    value = pool[places_s[k, body]]
                    straight = straight + factor[body, 2 * k] * value
                    turned = turned + factor[body, 2 * k + 1] * value
                incoming[team, body] = straight + turn(turned)

    def share_parts(team):
        bodies = [incoming[team, body] for body in range(BDEV)]

        @pl.loop(0, SITES // 8)
        def _(eight):
            for i in range(8):
                item = eight * 8 + i
                share = member[item, 0:1, :] * bodies[0]
                for body in range(1, BDEV):
                    share = share + member[item, body : body + 1, :] * bodies[body]
                shares[team, item] = share

        for dx in range(1, NX):
            send(
                shares.at[team, pl.ds(dx * NZ, NZ)],
                aside_parts.at[team, pl.ds(dx * NZ, NZ)],
                part_sems.at[0, team],
                part_sems.at[1, team],
                at(0, dx),
            )

    def share_totals(team):
        done(aside_parts.at[team, pl.ds(NZ, SITES - NZ)], part_sems.at[1, team])
        total = shares[team, pl.ds(0, NZ)]
        for dx in range(1, NX):
            total = total + aside_parts[team, pl.ds(dx * NZ, NZ)]
        totals[team, 0] = total
        for dz in range(1, NZ):
            send(
                totals.at[team, 0, dz],
                totals.at[team, 1, dz],
                share_sems.at[0, team],
                share_sems.at[1, team],
                at(dz, 0),
            )

    def store_coefficients(team):
        rows = product(to_rows(incoming[team]), d_hi, d_lo)
        for body, tile in enumerate(to_tiles(rows)):
            coef_out[body, team] = tile

    barrier = pltpu.get_barrier_semaphore()

    for step in range(1, SITES):
        site = at(step // NX, step % NX)
        pl.semaphore_signal(barrier, inc=1, device_id={"site": site}, device_id_type=MESH)

    loads = [
        pltpu.make_async_copy(src, dst, in_sems.at[i])
        for i, (src, dst) in enumerate(
            (
                (incident_h, incident),
                (diffraction_h, diffraction_v),
                (mixing_h, mixing_v),
                (coupling_h, coupling_v),
                (jacket_h, jacket_v),
                (lists_h, lists),
                (groups_h, groups),
            )
        )
    ]
    for load in loads:
        load.start()

    loads[1].wait()
    load_matrix(diffraction_v, d_hi, d_lo)
    loads[2].wait()
    load_matrix(mixing_v, m_hi, m_lo)
    loads[0].wait()
    for team in range(TEAMS):
        outgoing_of(0, team, incident[:, team])

    loads[5].wait()
    own_list = lists[...]
    owner = own_list // BDEV
    local = own_list % BDEV
    sites = lax.broadcasted_iota(jnp.int32, (SITES, K, BDEV), 0)
    named = owner[None] == sites
    last = jnp.where(named, local[None], -1)
    last = jnp.max(jnp.max(last, axis=1, keepdims=True), axis=2, keepdims=True)
    later = jnp.max(jnp.where(named & (local[None] == last), 1, 0), axis=0)
    behind = (z - owner // NX + NZ) % NZ
    aside = (x - owner % NX + NX) % NX
    places[...] = jnp.zeros((K, 128), jnp.int32)
    places[:, :BDEV] = jnp.where(owner == me, 2 * SITES + local, 2 * place_of(behind, aside) + later)
    move_places = pltpu.make_async_copy(places, places_s, table_sem.at[0])
    move_places.start()
    lists_all[0] = own_list

    loads[3].wait()
    real = is_real((ROWS, LANES))

    @pl.loop(0, BDEV)
    def _(body):
        for k in range(K):
            both = coupling_v[body, k]
            factor[body, 2 * k] = jnp.where(real, both, pltpu.roll(both, 1, 0))
            factor[body, 2 * k + 1] = jnp.where(real, pltpu.roll(both, ROWS - 1, 0), both)

    loads[4].wait()
    load_matrix(jacket_v, j_hi, j_lo)
    halves = []
    for part in range(2):
        columns = pl.ds(part * M, M)
        both = jnp.dot(d_hi[:, columns], j_hi[...], preferred_element_type=F32)
        both = both + jnp.dot(d_lo[:, columns], j_hi[...], preferred_element_type=F32)
        halves.append(both + jnp.dot(d_hi[:, columns], j_lo[...], preferred_element_type=F32))
    joint_real = halves[0][:, :NF] - halves[1][:, NF:]
    joint_imag = halves[0][:, NF:] + halves[1][:, :NF]
    j_hi[:, :NF], j_lo[:, :NF] = split(joint_real)
    j_hi[:, NF:], j_lo[:, NF:] = split(joint_imag)

    loads[6].wait()
    for body in range(BDEV):
        named_by[body : body + 1, :] = jnp.full((1, LANES), groups[0, body], jnp.int32)

    for item in range(SITES):
        member[item] = jnp.where(named_by[...] == at(item % NZ, item // NZ), 1.0, 0.0)

    pl.semaphore_wait(barrier, SITES - 1)

    send_dense(0, 0)
    for step in range(1, SITES):
        dz, dx = step // NX, step % NX
        send(
            lists,
            lists_all.at[((NZ - dz) % NZ) * NX + (NX - dx) % NX],
            list_sems.at[0],
            list_sems.at[1],
            at(dz, dx),
        )

    for team in range(1, TEAMS):
        send_dense(0, team)

    done(lists_all.at[1:], list_sems.at[1])
    everyone = lists_all[...]
    lane = lax.broadcasted_iota(jnp.int32, (SITES, 128), 1)
    table = jnp.zeros((SITES, 128), jnp.int32)
    for i, dz in enumerate((0, -1, 1, -2, 2)):
        theirs = everyone // BDEV == at(dz, 0)
        wanted = everyone % BDEV
        smallest = jnp.min(jnp.where(theirs, wanted, BDEV - 1), axis=1)
        largest = jnp.max(jnp.where(theirs, wanted, 0), axis=1)
        table = jnp.where(lane == 2 * i, jnp.min(smallest, axis=1, keepdims=True), table)
        table = jnp.where(lane == 2 * i + 1, jnp.max(largest, axis=1, keepdims=True), table)
    picks[...] = table
    move_picks = pltpu.make_async_copy(picks, picks_s, table_sem.at[1])
    move_picks.start()
    move_places.wait()
    move_picks.wait()

    for sweep in range(ITERS):
        if sweep == 0:
            for team in range(TEAMS):
                send_aside(sweep, team)
        for team in range(TEAMS):
            pass_near(sweep, team)
        for team in range(TEAMS):
            pass_far(sweep, team)
        if sweep < ITERS - 1:
            for team in range(TEAMS):
                gather(sweep, team)
                outgoing_of(sweep + 1, team, incoming[team])
                send_dense(sweep + 1, team)
                send_aside(sweep + 1, team)

    for team in range(TEAMS):
        gather(ITERS - 1, team)
        share_parts(team)
        if team > 0:
            share_totals(team - 1)
        store_coefficients(team)
    share_totals(TEAMS - 1)

    sums = []
    for team in range(TEAMS):
        done(totals.at[team, 1, pl.ds(1, NZ - 1)], share_sems.at[1, team])
        total = totals[team, 0, 0]
        for dz in range(1, NZ):
            total = total + totals[team, 1, dz]
        sums.append(total[None])
    total = jnp.concatenate(transpose_quads(sums), axis=-1)[0]
    resp_out[...] = product(total, j_hi, j_lo)

    done(lists_all.at[1:], list_sems.at[0])
    for team in range(TEAMS):
        for sweep in range(ITERS):
            for way in range(2):
                done(own.at[sweep, team], dense_send.at[sweep, team])
                done(near[sweep][team][way], dense_send.at[sweep, team])
            done(sending.at[sweep, team, pl.ds(LOCAL, 2 * SITES - LOCAL)], row_send.at[sweep, team])
        done(shares.at[team, pl.ds(NZ, SITES - NZ)], part_sems.at[0, team])
        done(totals.at[team, 0, pl.ds(1, NZ - 1)], share_sems.at[0, team])


def to_native(values):
    lead = values.shape[:-2]
    return jnp.swapaxes(values.reshape(*lead, 2, QUADS, LANES), -3, -2).reshape(*lead, ROWS, LANES)


def from_native(tiles):
    lead = tiles.shape[:-2]
    return jnp.swapaxes(tiles.reshape(*lead, QUADS, 2, LANES), -3, -2).reshape(*lead, 2, M)


def per_device(incident, diffraction, mixing, coupling, lists, groups, jacket):
    vmem = pl.BlockSpec(memory_space=pltpu.VMEM)
    anywhere = pl.BlockSpec(memory_space=pl.ANY)

    def f32(*shape):
        return pltpu.VMEM(shape, F32)

    def i32(*shape):
        return pltpu.VMEM(shape, jnp.int32)

    def dma(*shape):
        return pltpu.SemaphoreType.DMA(shape)

    coef, resp = pl.pallas_call(
        kernel,
        out_shape=(
            jax.ShapeDtypeStruct((BDEV, TEAMS, ROWS, LANES), F32),
            jax.ShapeDtypeStruct((ROWS, NF), F32),
        ),
        in_specs=[anywhere] * 7,
        out_specs=(vmem, vmem),
        scratch_shapes=[
            f32(BDEV, TEAMS, ROWS, LANES),
            f32(2, M, M),
            f32(2, M, M),
            f32(BDEV, K, ROWS, LANES),
            f32(2, M, NF),
            i32(K, BDEV),
            pltpu.SMEM((1, BDEV), jnp.int32),
            *[pltpu.VMEM((M, 2 * M), BF16)] * 4,
            *[pltpu.VMEM((M, 2 * NF), BF16)] * 2,
            f32(BDEV, 2 * K, ROWS, LANES),
            f32(TEAMS, BDEV, ROWS, LANES),
            f32(ITERS, TEAMS, BDEV, ROWS, LANES),
            i32(SITES, K, BDEV),
            i32(SITES, 128),
            i32(K, 128),
            i32(BDEV, LANES),
            f32(SITES, BDEV, LANES),
            pltpu.SMEM((SITES, 128), jnp.int32),
            pltpu.SMEM((K, 128), jnp.int32),
            f32(ITERS, TEAMS, 2 * SITES, ROWS, LANES),
            f32(TEAMS, SITES, ROWS, LANES),
            f32(TEAMS, SITES, ROWS, LANES),
            f32(TEAMS, 2, NZ, ROWS, LANES),
            *[f32(POOL, ROWS, LANES)] * (ITERS * TEAMS),
            *[f32(BDEV, ROWS, LANES)] * (ITERS * TEAMS * 4),
            dma(7),
            dma(2),
            dma(ITERS, TEAMS),
            dma(ITERS, TEAMS, 2),
            dma(ITERS, TEAMS, 2),
            dma(ITERS, TEAMS),
            dma(ITERS, TEAMS),
            dma(2, TEAMS),
            dma(2, TEAMS),
            dma(2),
        ],
        compiler_params=pltpu.CompilerParams(
            collective_id=0, has_side_effects=True, vmem_limit_bytes=44 * 1024 * 1024
        ),
        cost_estimate=pl.CostEstimate(
            flops=3_000_000_000, bytes_accessed=6_000_000, transcendentals=0
        ),
    )(
        *[
            pltpu.with_memory_space_constraint(operand, pltpu.HBM)
            for operand in (
                to_native(incident),
                diffraction,
                mixing,
                to_native(coupling),
                lists.T,
                groups.reshape(1, BDEV),
                jacket.reshape(2, M, NF),
            )
        ]
    )
    return from_native(coef), resp.reshape(1, 4, 2, NF)


def solution(mesh):
    placed = (
        P("site", "freq", None, None),
        P("freq", None, None),
        P("freq", None, None),
        P("site", "freq", None, None),
        P("site", None),
        P("site", None),
        P("site", "freq", None, None),
    )
    return jax.shard_map(
        per_device,
        mesh=mesh,
        in_specs=placed,
        out_specs=(P("site", "freq", None, None), P("site", "freq", None, None)),
        check_vma=False,
    )
```

time: 91.3 us -> 87.6 us (0.959)
  local copies, waits for them, and re-layouts: 6.52 us -> 1.3 us
  Pallas kernels: 83.4 us -> 85.5 us
    reshape x4 -> x0, local copies, waits for them, and re-layouts: 3.47 us -> none  [the longest x1 1.4 us: per_device(): coupling.reshape(BDEV, 2 * K, M)]
    pallas_call x1, Pallas kernels: 83.4 us -> 85.5 us  [per_device(): pl.pallas_call(kernel, out_shape=(jax.ShapeDtypeStruct((BDEV, TEAMS, ROWS...]
    unnamed x6 -> x2, local copies, waits for them, and re-layouts: 3.04 us -> 1.3 us
where the time goes in v3:
time: 87.6 us; the launch traced here: 87.5 us
  Pallas kernels  85.5 us (98%)
  local copies, waits for them, and re-layouts  1.3 us (1%)
    pallas_call x1, Pallas kernels, per_device(): pl.pallas_call(kernel, out_shape=(jax.ShapeDtypeStruct((BDEV, TEAMS, ROWS...  85.5 us

profile of v3, /device:TPU:8, one launch (start us, length us, event | category | flops | bytes accessed | tf_op | source)
XLA Modules:
  0.0 87.5 jit_solution(10756177358841772776)
XLA Ops:
  0.6 85.5 %shard_map.86 = (f32[16,4,8,128]{3,2,1,0:T(8,128)S(1)}, f32[8,128]{1,0:T(8,128)S(1)}) custom-call(f32[16,4,8,128]{3,2,1,0:T(8,128)} %bitcast.23, f32[2,512,512]{2,1,0:T(8,128)} %refs_1_.1, f32[2,512,512]{2,1,0:T(8,128)} %refs_2_.1, f32[16,8,8,128]{3,2,1,0:T(8,128)} %bitcast.21, s32[8,16]{1,0:T(8,128)} %bitcast.24, s32[1,16]{1,0:T(1,128)} %bitcast.25, ...), custom_call_target="tpu_custom_call" | custom-call | flops 3000000000 | bytes 6000000 | tf_op jit(solution)/shard_map/pallas_call | solution.py:436
  86.2 0.7 copy.14
  86.9 0.6 copy.15

commit v4 on v3

--- a/solution.py
+++ b/solution.py
@@ -143,11 +143,14 @@
                 at(step, 0),
             )
 
-    def send_picked(sweep, team, block, dz, dx, behind, lane, number, skip):
+    def pick(sweep, team, block, dz, dx, behind, lane, number, skip):
         row = 2 * place_of((behind + NZ) % NZ, dx) + skip
         entry = ((dz + NZ) % NZ) * NX + dx
         for i in range(number):
             sending[sweep, team, row + i] = block[picks_s[entry, lane + skip + i]]
+        return row
+
+    def send_rows(sweep, team, row, number, dz, dx):
         send(
             sending.at[sweep, team, pl.ds(row, number)],
             pools[sweep][team].at[pl.ds(row, number)],
@@ -156,9 +159,9 @@
             at(dz, dx),
         )
 
-    def send_aside(sweep, team):
+    def pick_aside(sweep, team):
         for dx in range(1, NX):
-            send_picked(sweep, team, own.at[sweep, team], 0, dx, 0, 0, 2, 0)
+            pick(sweep, team, own.at[sweep, team], 0, dx, 0, 0, 2, 0)
 
     def pass_near(sweep, team):
         for way, step in enumerate(WAYS):
@@ -171,24 +174,33 @@
                 at(step, 0),
             )
 
+    def pick_near(sweep, team):
         for dx in range(1, NX):
             for way, step in enumerate(WAYS):
-                send_picked(sweep, team, near[sweep][team][way], 0, dx, step, 2 + 2 * way, 2, 0)
+                pick(sweep, team, near[sweep][team][way], 0, dx, step, 2 + 2 * way, 2, 0)
+            send_rows(sweep, team, 2 * place_of(NZ - 1, dx), 6, 0, dx)
 
     def pass_far(sweep, team):
         for way in range(2):
             done(far[sweep][team][way], far_recv.at[sweep, team, way])
 
-        for dx in range(NX):
-            for way, step in enumerate(WAYS):
-                send_picked(sweep, team, far[sweep][team][way], 2 * step, dx, 4 * step, 6 + 2 * way, 1, way)
-
-        for item in range(2 * NX - 1, 0, -1):
-            hop, dx = item // NX, item % NX
-            for way, step in enumerate(WAYS):
-                send_picked(
-                    sweep, team, far[sweep][team][way], step * hop, dx, step * (hop + 2), 6 + 2 * way, 2, 0
-                )
+        for hop, number in ((2, 1), (0, 2), (1, 2)):
+            for dx in range(NX):
+                for way, step in enumerate(WAYS):
+                    if hop > 0 or dx > 0:
+                        skip = way if hop == 2 else 0
+                        row = pick(
+                            sweep,
+                            team,
+                            far[sweep][team][way],
+                            step * hop,
+                            dx,
+                            step * (hop + 2),
+                            6 + 2 * way,
+                            number,
+                            skip,
+                        )
+                        send_rows(sweep, team, row, number, step * hop, dx)
 
         pool = pools[sweep][team]
         pool[2 * SITES :] = own[sweep, team]
@@ -226,6 +238,19 @@
                     share = share + member[item, body : body + 1, :] * bodies[body]
                 shares[team, item] = share
 
+        if team == TEAMS - 1:
+            for dz in (4, 3, 5, 2, 6, 1, 7, 0):
+                for dx in range(NX):
+                    item = dx * NZ + dz
+                    if item > 0:
+                        send(
+                            shares.at[team, item],
+                            aside_parts.at[team, item],
+                            part_sems.at[0, team],
+                            part_sems.at[1, team],
+                            at(dz, dx),
+                        )
+            return
         for dx in range(1, NX):
             send(
                 shares.at[team, pl.ds(dx * NZ, NZ)],
@@ -369,9 +394,10 @@
     for sweep in range(ITERS):
         if sweep == 0:
             for team in range(TEAMS):
-                send_aside(sweep, team)
+                pick_aside(sweep, team)
         for team in range(TEAMS):
             pass_near(sweep, team)
+            pick_near(sweep, team)
         for team in range(TEAMS):
             pass_far(sweep, team)
         if sweep < ITERS - 1:
@@ -379,7 +405,7 @@
                 gather(sweep, team)
                 outgoing_of(sweep + 1, team, incoming[team])
                 send_dense(sweep + 1, team)
-                send_aside(sweep + 1, team)
+                pick_aside(sweep + 1, team)
 
     for team in range(TEAMS):
         gather(ITERS - 1, team)
@@ -387,10 +413,30 @@
         if team > 0:
             share_totals(team - 1)
         store_coefficients(team)
-    share_totals(TEAMS - 1)
+
+    done(lists_all.at[1:], list_sems.at[0])
+    for sweep in range(ITERS):
+        for team in range(TEAMS):
+            done(own.at[sweep], dense_send.at[sweep, team])
+            done(sending.at[sweep, team, pl.ds(LOCAL, 2 * SITES - LOCAL)], row_send.at[sweep, team])
+
+    def done_sums():
+        for team in range(TEAMS):
+            if team == TEAMS - 1:
+                done(shares.at[team, pl.ds(1, SITES - 1)], part_sems.at[0, team])
+                continue
+            done(shares.at[team, pl.ds(NZ, SITES - NZ)], part_sems.at[0, team])
+            done(totals.at[team, 0, pl.ds(1, NZ - 1)], share_sems.at[0, team])
 
     sums = []
     for team in range(TEAMS):
+        if team == TEAMS - 1:
+            done(aside_parts.at[team, pl.ds(1, SITES - 1)], part_sems.at[1, team])
+            parts = [shares[team, 0]] + [aside_parts[team, item] for item in range(1, SITES)]
+            while len(parts) > 1:
+                parts = [a + b for a, b in zip(parts[::2], parts[1::2])]
+            sums.append(parts[0][None])
+            continue
         done(totals.at[team, 1, pl.ds(1, NZ - 1)], share_sems.at[1, team])
         total = totals[team, 0, 0]
         for dz in range(1, NZ):
@@ -398,16 +444,7 @@
         sums.append(total[None])
     total = jnp.concatenate(transpose_quads(sums), axis=-1)[0]
     resp_out[...] = product(total, j_hi, j_lo)
-
-    done(lists_all.at[1:], list_sems.at[0])
-    for team in range(TEAMS):
-        for sweep in range(ITERS):
-            for way in range(2):
-                done(own.at[sweep, team], dense_send.at[sweep, team])
-                done(near[sweep][team][way], dense_send.at[sweep, team])
-            done(sending.at[sweep, team, pl.ds(LOCAL, 2 * SITES - LOCAL)], row_send.at[sweep, team])
-        done(shares.at[team, pl.ds(NZ, SITES - NZ)], part_sems.at[0, team])
-        done(totals.at[team, 0, pl.ds(1, NZ - 1)], share_sems.at[0, team])
+    done_sums()
 
 
 def to_native(values):

time: 87.6 us -> 87.1 us (level)
  no operation moved by 1% of the time
where the time goes in v4:
time: 87.1 us; the launch traced here: 87 us
  Pallas kernels  85.1 us (98%)
  local copies, waits for them, and re-layouts  1.3 us (1%)
    pallas_call x1, Pallas kernels, per_device(): pl.pallas_call(kernel, out_shape=(jax.ShapeDtypeStruct((BDEV, TEAMS, ROWS...  85.1 us

profile of v4, /device:TPU:8, one launch (start us, length us, event | category | flops | bytes accessed | tf_op | source)
XLA Modules:
  0.0 87.0 jit_solution(2856886408793763289)
XLA Ops:
  0.6 85.1 %shard_map.86 = (f32[16,4,8,128]{3,2,1,0:T(8,128)S(1)}, f32[8,128]{1,0:T(8,128)S(1)}) custom-call(f32[16,4,8,128]{3,2,1,0:T(8,128)} %bitcast.23, f32[2,512,512]{2,1,0:T(8,128)} %refs_1_.1, f32[2,512,512]{2,1,0:T(8,128)} %refs_2_.1, f32[16,8,8,128]{3,2,1,0:T(8,128)} %bitcast.21, s32[8,16]{1,0:T(8,128)} %bitcast.24, s32[1,16]{1,0:T(1,128)} %bitcast.25, ...), custom_call_target="tpu_custom_call" | custom-call | flops 3000000000 | bytes 6000000 | tf_op jit(solution)/shard_map/pallas_call | solution.py:473
  85.7 0.7 copy.14
  86.4 0.6 copy.15

commit v5 on v4

--- a/solution.py
+++ b/solution.py
@@ -392,11 +392,9 @@
     move_picks.wait()
 
     for sweep in range(ITERS):
-        if sweep == 0:
-            for team in range(TEAMS):
-                pick_aside(sweep, team)
         for team in range(TEAMS):
             pass_near(sweep, team)
+            pick_aside(sweep, team)
             pick_near(sweep, team)
         for team in range(TEAMS):
             pass_far(sweep, team)
@@ -405,7 +403,6 @@
                 gather(sweep, team)
                 outgoing_of(sweep + 1, team, incoming[team])
                 send_dense(sweep + 1, team)
-                pick_aside(sweep + 1, team)
 
     for team in range(TEAMS):
         gather(ITERS - 1, team)

time: 87.1 us -> 87.2 us (level)
  no operation moved by 1% of the time
where the time goes in v5:
time: 87.2 us; the launch traced here: 87.1 us
  Pallas kernels  85.2 us (98%)
  local copies, waits for them, and re-layouts  1.3 us (1%)
    pallas_call x1, Pallas kernels, per_device(): pl.pallas_call(kernel, out_shape=(jax.ShapeDtypeStruct((BDEV, TEAMS, ROWS...  85.2 us

profile of v5, /device:TPU:8, one launch (start us, length us, event | category | flops | bytes accessed | tf_op | source)
XLA Modules:
  0.0 87.1 jit_solution(4585344934655528303)
XLA Ops:
  0.6 85.2 %shard_map.86 = (f32[16,4,8,128]{3,2,1,0:T(8,128)S(1)}, f32[8,128]{1,0:T(8,128)S(1)}) custom-call(f32[16,4,8,128]{3,2,1,0:T(8,128)} %bitcast.23, f32[2,512,512]{2,1,0:T(8,128)} %refs_1_.1, f32[2,512,512]{2,1,0:T(8,128)} %refs_2_.1, f32[16,8,8,128]{3,2,1,0:T(8,128)} %bitcast.21, s32[8,16]{1,0:T(8,128)} %bitcast.24, s32[1,16]{1,0:T(1,128)} %bitcast.25, ...), custom_call_target="tpu_custom_call" | custom-call | flops 3000000000 | bytes 6000000 | tf_op jit(solution)/shard_map/pallas_call | solution.py:470
  85.8 0.7 copy.14
  86.5 0.6 copy.15
